TPU v7x, 32 devices: a whole 2x2x4 slice. The times are simulated.
32 devices in a mesh: sec: 2 (over y), ty: 16 (over z, x, core).
Axes of the slice: x: 2, y: 2, z: 4, core: 2. Of those that a mesh axis runs over, the one named last changes fastest.
Arguments:
- points: float32 [4, 32768], P(None, ('sec', 'ty')), parts along dimension 1, may hold values from -88 to 2136, as said below
- source: bfloat16 [1024, 2048], P(('sec', 'ty')), parts along dimension 0, may hold values from -4 to 4
- slab_first: int32 [32], P(('sec', 'ty')), parts along dimension 0, may hold values from 0 to 29, as said below
- slab_count: int32 [32], P(('sec', 'ty')), parts along dimension 0, may hold values from 3 to 6, as said below
Outputs:
- rendered: bfloat16 [1024, 2048], P(('sec', 'ty')), parts along dimension 0
- vertex_affines: float32 [6, 128, 256], P(None, ('sec', 'ty')), parts along dimension 1
There are 2 independent parts, one for each index of `sec`. A program takes and returns all parts, laid end to end along the dimension named above; each array names one. Nothing has to cross between parts.
Inputs may be any that keep to these rules, and one draw needn't show every extreme that they name: `points`: for tile t, rows 0 and 1 are fixed positions: each 16 x 16 pixel cell of rows t*32 to (t+1)*32 and columns 0 to 2048 holds 4 of them, listed cell by cell, cells in row-major order; rows 2 and 3 are the matching moving positions. Source block j is rows j*16 to (j+1)*16 - 1. Tile t samples blocks slab_first[t] to slab_first[t] + slab_count[t] - 1, all within rows (t-1)*32 to (t+2)*32 - 1. slab_count reaches 6 on some tile in every draw.
All inputs are finite; a program needn't handle non-finite values.
Results may differ from a plain program's by a relative error of at most 0.008.
Values may be sent and summed in bfloat16 or wider, within the bound.
No kernel may reach another device: no remote copies, remote signals or barrier semaphores. Data moves between devices by JAX's collectives and lax.ppermute only.
A program may use at most 64 MiB of HBM per device.

v0:
```python
import functools

import jax
import jax.numpy as jnp
import numpy as np
from jax import lax
from jax.experimental import pallas as pl
from jax.experimental.pallas import tpu as pltpu
from jax.sharding import PartitionSpec as P

BH = 16
PC = 4
SP = 8
VR = 4
LANES = 128
CELL = 16
RIDGE_TERM = 0.01
FEATS = 12
ER = 8
NF = FEATS * ER
GROUP_PX = LANES // PC * CELL
NV = GROUP_PX // SP + 2 * LANES // SP
EXP2_SCALE = 2.0 * float(np.log2(np.e))
TAPS = 12


def fiota(shape, dim):
    return lax.broadcasted_iota(jnp.int32, shape, dim).astype(jnp.float32)


def local_points(pts, tile, cell_cols, height):
    lane = lax.broadcasted_iota(jnp.int32, (1, pts.shape[1]), 1)
    cell = lane // PC
    base_x = (cell % cell_cols * CELL).astype(jnp.float32)
    base_y = (tile * height + cell // cell_cols * CELL).astype(jnp.float32)
    fixed_x, fixed_y = pts[0:1], pts[1:2]
    return jnp.concatenate(
        [fixed_x - base_x, fixed_y - base_y, pts[2:3] - fixed_x, pts[3:4] - fixed_y], axis=0
    )


def lookup(values, index):
    numbers = lax.GatherDimensionNumbers(
        offset_dims=(),
        collapsed_slice_dims=(1,),
        start_index_map=(1,),
        operand_batching_dims=(0,),
        start_indices_batching_dims=(0,),
    )
    return lax.gather(values, index[..., None], numbers, (1, 1), mode=lax.GatherScatterMode.PROMISE_IN_BOUNDS)


def split_pair(value):
    high = value.astype(jnp.bfloat16).astype(jnp.float32)
    return high, value - high


def lay_source_kernel(source_ref, packed_ref):
    height, width = source_ref.shape
    half = packed_ref.shape[1]
    for part in range(width // half):
        packed_ref[part * height : (part + 1) * height, :] = source_ref[:, part * half : (part + 1) * half]


def lay_points_kernel(height, width, own_ref, mate_ref, laid_ref, packed_ref, rows_ref, sem):
    tile = lax.axis_index("ty")
    rows = []
    for ref, owner in ((own_ref, tile), (mate_ref, tile + 1 - 2 * (tile % 2))):
        rows.extend(split_pair(local_points(ref[...], owner, width // CELL, height)))
    rows_ref[...] = jnp.concatenate(rows, axis=0).astype(jnp.bfloat16)
    base = packed_ref.shape[0] - 16
    copy = pltpu.make_async_copy(rows_ref, packed_ref.at[base : base + 16, :], sem)
    copy.start()
    copy.wait()


def group_totals(sets, tile, strips, height, width, feat_ref, weight_ref):
    cell_cols = width // CELL
    cell_rows = height // CELL
    groups = width // GROUP_PX
    ext_row = lax.broadcasted_iota(jnp.int32, (ER, 1), 0)
    vertex_y = (fiota((ER, 1), 0) * SP + (SP / 2.0 - SP - height / 2.0)) / height
    ext_tile = tile + jnp.where(ext_row == 0, -1, jnp.where(ext_row == VR + 1, 1, 0))
    scale = float(np.sqrt(EXP2_SCALE))
    lane_px = (lax.broadcasted_iota(jnp.int32, (1, LANES), 1) // PC * CELL).astype(jnp.float32) - GROUP_PX / 2.0
    vertex_ids = lax.broadcasted_iota(jnp.int32, (NV, LANES), 0)
    point_block = lax.broadcasted_iota(jnp.int32, (NV, LANES), 1) // (LANES // CELL * PC)
    band = (jnp.abs(vertex_ids // (LANES // SP) - 1 - point_block) <= 1).astype(jnp.float32)
    vertex_scaled = (fiota((NV, 1), 0) * SP + (SP / 2.0 - LANES - GROUP_PX / 2.0)) * (scale / height)
    zero_rows = jnp.zeros((LANES - NV, weight_ref.shape[2]), jnp.bfloat16)

    totals = []
    for g in range(groups):
        weight_ref[g, NV:LANES, :] = zero_rows
        weight_ref[g, LANES + NV :, :] = zero_rows
        for s, (pts, owner) in enumerate(sets):
            usable = (jnp.abs(owner - ext_tile) <= 1) & (owner >= 0) & (owner < strips)
            usable = usable.astype(jnp.float32)
            for c in range(cell_rows):
                lanes = slice(c * cell_cols * PC + g * LANES, c * cell_cols * PC + (g + 1) * LANES)
                chunk = slice((s * cell_rows + c) * LANES, (s * cell_rows + c + 1) * LANES)
                px = (pts[0:1, lanes] + lane_px) / height
                py = (pts[1:2, lanes] + ((owner - tile) * height + c * CELL).astype(jnp.float32)) / height - 0.5
                dx = pts[2:3, lanes] / height
                dy = pts[3:4, lanes] / height
                gap_y = (py - vertex_y) * scale
                wy = jnp.exp2(-(gap_y * gap_y)) * usable
                wpx, wpy, wdx, wdy = wy * px, wy * py, wy * dx, wy * dy
                rows = (wy, wpx, wpy, wdx, wdy, wpx * px, wpx * py, wpy * py, wdx * px, wdx * py, wdy * px, wdy * py)
                for f in range(0, FEATS, 2):
                    high, low = split_pair(jnp.concatenate(rows[f : f + 2], axis=0))
                    feat_ref[g, f * ER : (f + 2) * ER, chunk] = high.astype(jnp.bfloat16)
                    feat_ref[g, NF + f * ER : NF + (f + 2) * ER, chunk] = low.astype(jnp.bfloat16)
                gap_x = px * scale - vertex_scaled
                wx = jnp.exp2(-(gap_x * gap_x)) * band
                high, low = split_pair(wx)
                weight_ref[g, 0:NV, chunk] = high.astype(jnp.bfloat16)
                weight_ref[g, LANES : LANES + NV, chunk] = low.astype(jnp.bfloat16)
        both = lax.dot_general(
            feat_ref[g], weight_ref[g], (((1,), (1,)), ((), ())), preferred_element_type=jnp.float32
        )
        both = both[:NF] + both[NF:]
        totals.append(both[:, :LANES] + both[:, LANES:])
    return totals


def near_kernel(strips, height, width, own_ref, mate_ref, totals_ref, feat_ref, weight_ref):
    tile = lax.axis_index("ty")
    mate = tile + 1 - 2 * (tile % 2)
    cell_cols = width // CELL
    sets = (
        (local_points(own_ref[...], tile, cell_cols, height), tile),
        (local_points(mate_ref[...], mate, cell_cols, height), mate),
    )
    for g, value in enumerate(group_totals(sets, tile, strips, height, width, feat_ref, weight_ref)):
        totals_ref[g] = value


def main_kernel(
    strips,
    first_ref,
    count_ref,
    totals_ref,
    source_ref,
    mate_source_ref,
    packed_ref,
    far_ref,
    out_ref,
    affine_ref,
    feat_ref,
    weight_ref,
    slab_ref,
    sample_ref,
    base_ref,
    span_ref,
    taken_ref,
    mixed_ref,
    widest_ref,
):
    height, width = source_ref.shape
    groups = width // GROUP_PX
    blocks = width // LANES
    halves = blocks // 8
    tile = lax.axis_index("ty")
    odd = tile % 2
    toward = 1 - 2 * odd
    partner = tile - toward
    partner_mate = tile - 2 * toward
    beyond = tile + 2 * toward

    slots_from = first_ref[0] * BH - (tile - 1) * height
    slots_to = slots_from + count_ref[0] * BH
    left_half = lax.broadcasted_iota(jnp.int32, (1, LANES), 1) < LANES // 2
    half_cols = packed_ref.shape[1]
    slab_ref[3 * height :, :] = jnp.zeros((slab_ref.shape[0] - 3 * height, slab_ref.shape[1]), jnp.bfloat16)

    def place(load, row_start, chunk):
        local = row_start + chunk * 16
        row = lax.broadcasted_iota(jnp.int32, (16, 1), 0) + local
        live = ((row >= slots_from) & (row < slots_to)).astype(jnp.float32)
        before = jnp.zeros((16, LANES), jnp.float32)
        for b in range(blocks + 1):
            if b < blocks:
                now = pltpu.roll(load(b).astype(jnp.float32) * live, LANES // 2, axis=1)
            else:
                now = jnp.zeros((16, LANES), jnp.float32)
            merged = jnp.where(left_half, before, now).astype(jnp.bfloat16)
            slab_ref[pl.ds(pl.multiple_of(local, 16), 16), b * LANES : (b + 1) * LANES] = merged
            before = now

    for chunk in range(height // 16):
        rows = slice(chunk * 16, chunk * 16 + 16)
        place(lambda b: source_ref[rows, b * LANES : (b + 1) * LANES], height, chunk)
        place(lambda b: mate_source_ref[rows, b * LANES : (b + 1) * LANES], height + toward * height, chunk)

        def from_packed(b):
            part = b * LANES // half_cols
            lane = b * LANES - part * half_cols
            return packed_ref[part * height + chunk * 16 : part * height + chunk * 16 + 16, lane : lane + LANES]

        place(from_packed, height - toward * height, chunk)

    point_rows = packed_ref[packed_ref.shape[0] - 16 :, :].astype(jnp.float32)
    far_rows = far_ref[...].astype(jnp.float32)
    sets = (
        (point_rows[0:4] + point_rows[4:8], partner),
        (point_rows[8:12] + point_rows[12:16], partner_mate),
        (far_rows[0:4] + far_rows[4:8], beyond),
    )
    vertex_y = (fiota((ER, 1), 0) * SP + (SP / 2.0 - SP - height / 2.0)) / height
    totals = group_totals(sets, tile, strips, height, width, feat_ref, weight_ref)
    totals = [totals[g] + totals_ref[g] for g in range(groups)]

    lane = lax.broadcasted_iota(jnp.int32, (1, LANES), 1)
    per_group = GROUP_PX // SP
    affines = []
    for h in range(halves):
        moments = None
        vertex_group = 2 * h + lane // per_group
        for g in range(groups):
            start = g * per_group - LANES // SP - h * LANES
            if start + NV <= 0 or start >= LANES:
                continue
            part = pltpu.roll(totals[g], start % LANES, axis=1)
            inside = ((lane >= start) & (lane < start + NV)).astype(jnp.float32)
            move = ((g - vertex_group) * (GROUP_PX // height)).astype(jnp.float32)
            part = [part[f * ER : (f + 1) * ER] * inside for f in range(FEATS)]
            part[5] = part[5] + move * (2.0 * part[1] + move * part[0])
            part[6] = part[6] + move * part[2]
            part[8] = part[8] + move * part[3]
            part[10] = part[10] + move * part[4]
            part[1] = part[1] + move * part[0]
            moments = part if moments is None else [x + y for x, y in zip(moments, part)]
        inverse = 1.0 / moments[0]
        mean_px, mean_py, mean_dx, mean_dy = [moments[i] * inverse for i in range(1, 5)]
        cov_xx = moments[5] * inverse - mean_px * mean_px + RIDGE_TERM
        cov_xy = moments[6] * inverse - mean_px * mean_py
        cov_yy = moments[7] * inverse - mean_py * mean_py + RIDGE_TERM
        cross_xx = moments[8] * inverse - mean_dx * mean_px - RIDGE_TERM
        cross_xy = moments[9] * inverse - mean_dx * mean_py
        cross_yx = moments[10] * inverse - mean_dy * mean_px
        cross_yy = moments[11] * inverse - mean_dy * mean_py - RIDGE_TERM
        over = 1.0 / (cov_xx * cov_yy - cov_xy * cov_xy)
        lin_xx = (cross_xx * cov_yy - cross_xy * cov_xy) * over
        lin_xy = (cross_xy * cov_xx - cross_xx * cov_xy) * over
        lin_yx = (cross_yx * cov_yy - cross_yy * cov_xy) * over
        lin_yy = (cross_yy * cov_xx - cross_yx * cov_xy) * over
        vertex_x = ((lane % per_group * SP).astype(jnp.float32) + (SP - GROUP_PX) / 2.0) / height
        delta_x = vertex_x - mean_px
        delta_y = vertex_y - mean_py
        shift_x = mean_dx + lin_xx * delta_x + lin_xy * delta_y
        shift_y = mean_dy + lin_yx * delta_x + lin_yy * delta_y
        results = (lin_xx + 1.0, lin_xy, lin_yx, lin_yy + 1.0, shift_x, shift_y)
        for i, value in enumerate(results):
            affine_ref[i, :, h * LANES : (h + 1) * LANES] = value[1 : VR + 1]
        affines.append((shift_x, shift_y))

    ext = lax.broadcasted_iota(jnp.int32, (ER, LANES), 0)
    along = (lane % SP).astype(jnp.float32) / SP - 0.5
    left_side = along < 0.0
    vertex_rows = []
    for comp in range(2):
        rows = []
        for h in range(halves):
            value = affines[h][comp] * float(height)
            value = jnp.where((ext == 0) & (tile == 0), jnp.broadcast_to(value[1:2], value.shape), value)
            value = jnp.where((ext == VR + 1) & (tile == strips - 1), jnp.broadcast_to(value[VR : VR + 1], value.shape), value)
            rows.append(value)
        steps = []
        for h in range(halves):
            value = rows[h]
            first = jnp.broadcast_to(rows[h - 1][:, LANES - 1 :] if h > 0 else value[:, :1], value.shape)
            last = jnp.broadcast_to(rows[h + 1][:, :1] if h + 1 < halves else value[:, LANES - 1 :], value.shape)
            before = jnp.where(lane == 0, first, pltpu.roll(value, 1, axis=1))
            after = jnp.where(lane == LANES - 1, last, pltpu.roll(value, LANES - 1, axis=1))
            steps.append((value, value - before, after - value))
        vertex_rows.append(steps)

    sub = lax.broadcasted_iota(jnp.int32, (8, LANES), 0).astype(jnp.float32)
    lane_full = fiota((8, LANES), 1)
    tents = (
        jnp.maximum(0.0, 0.5 - sub / SP),
        1.0 - jnp.abs(sub - SP / 2.0) / SP,
        jnp.maximum(0.0, sub / SP - 0.5),
    )
    last_row = 3.0 * height
    spans = None

    def clipped_floor(sample_y):
        return jnp.clip(jnp.floor(sample_y), -2.0, last_row)

    def one_hot(base, k, offset):
        return jnp.where(lane_full - base == float(offset), 1.0, 0.0)

    def tap_rows(bases, offset, slab):
        picks = [
            jnp.concatenate([one_hot(bases[k], k, offset + j) for k in range(len(bases))], axis=0).astype(jnp.bfloat16)
            for j in range(TAPS)
        ]
        return jnp.dot(jnp.concatenate(picks, axis=0), slab, preferred_element_type=jnp.float32).astype(jnp.bfloat16)

    def render(sample_x, sample_y, base, taken, k):
        floor_x = jnp.floor(sample_x)
        part_x = sample_x - floor_x
        part_y = sample_y - jnp.floor(sample_y)
        floor_x = jnp.clip(floor_x, -2.0, 2.0 * LANES)
        weight_0 = jnp.where((floor_x >= 0.0) & (floor_x < 2.0 * LANES), 1.0 - part_x, 0.0)
        weight_1 = jnp.where((floor_x >= -1.0) & (floor_x < 2.0 * LANES - 1.0), part_x, 0.0)
        index = floor_x.astype(jnp.int32)
        index_0 = (index & (LANES - 1)).astype(jnp.int16)
        index_1 = ((index + 1) & (LANES - 1)).astype(jnp.int16)
        index = index.astype(jnp.int16)
        in_0 = index < LANES
        in_1 = index < LANES - 1
        step = (clipped_floor(sample_y) - base).astype(jnp.int32).astype(jnp.int16)
        near, after = taken
        at = [slice(j * height + k * 16, j * height + k * 16 + 16) for j in range(TAPS)]
        near_0 = [lookup(near(i), index_0) for i in at]
        next_0 = [lookup(after(i), index_0) for i in at]
        near_1 = [lookup(near(i), index_1) for i in at]
        next_1 = [lookup(after(i), index_1) for i in at]
        top_0 = top_1 = low_0 = low_1 = jnp.zeros((16, LANES), jnp.bfloat16)
        before = step == -1
        for j in range(TAPS):
            value_0 = jnp.where(in_0, near_0[j], next_0[j])
            value_1 = jnp.where(in_1, near_1[j], next_1[j])
            here = step == j
            top_0 = jnp.where(here, value_0, top_0)
            top_1 = jnp.where(here, value_1, top_1)
            low_0 = jnp.where(before, value_0, low_0)
            low_1 = jnp.where(before, value_1, low_1)
            before = here
        upper = weight_0 * top_0.astype(jnp.float32) + weight_1 * top_1.astype(jnp.float32)
        lower = weight_0 * low_0.astype(jnp.float32) + weight_1 * low_1.astype(jnp.float32)
        return upper + part_y * (lower - upper)

    row_groups = height // 8
    block_spans = []
    for b in range(blocks):
        spread = (b % 8) * (LANES // SP) + lax.broadcasted_iota(jnp.int32, (8, LANES), 1) // SP
        expanded = []
        for comp in range(2):
            value, rise, climb = vertex_rows[comp][b // 8]
            at = jnp.take_along_axis(value, spread, axis=1)
            low = jnp.take_along_axis(rise, spread, axis=1)
            high = jnp.take_along_axis(climb, spread, axis=1)
            expanded.append(at + along * jnp.where(left_side, low, high))
        columns = slice(b * LANES, (b + 1) * LANES)
        span = None
        for k in range(row_groups):
            moved = [
                tents[0] * ex[k : k + 1] + tents[1] * ex[k + 1 : k + 2] + tents[2] * ex[k + 2 : k + 3] for ex in expanded
            ]
            sample_x = lane_full + (moved[0] + LANES / 2.0)
            sample_y = sub + (moved[1] + float(k * 8 + height))
            rows = slice(k * 8, k * 8 + 8)
            sample_ref[0, rows, columns] = sample_x
            sample_ref[1, rows, columns] = sample_y
            floor_y = clipped_floor(sample_y)
            base = jnp.min(floor_y, axis=1, keepdims=True)
            base_ref[b, rows, :] = jnp.broadcast_to(base, (8, LANES))
            span = floor_y - base if span is None else jnp.maximum(span, floor_y - base)
        span_ref[b] = span
        spans = span if spans is None else jnp.maximum(spans, span)

    for b in range(blocks):
        columns = slice(b * LANES, (b + 1) * LANES)
        bases = [base_ref[b, k * 8 : k * 8 + 8, :] for k in range(row_groups)]
        taken_ref[b] = tap_rows(bases, 0, slab_ref[:, b * LANES : (b + 2) * LANES])

    for b in range(blocks):
        columns = slice(b * LANES, (b + 1) * LANES)
        taken = (lambda i: taken_ref[b, i, :LANES]), (lambda i: taken_ref[b, i, LANES:])
        for k in range(height // 16):
            rows = slice(k * 16, k * 16 + 16)
            mixed_ref[rows, columns] = render(
                sample_ref[0, rows, columns], sample_ref[1, rows, columns], base_ref[b, rows, :], taken, k
            )

    @pl.when(jnp.max(spans) > TAPS - 2.0)
    def _():
        for b in range(blocks):
            widest_ref[b] = jnp.max(span_ref[b]).astype(jnp.int32)

        def rest(b, carry):
            widest = widest_ref[b]

            @pl.when(widest > TAPS - 2)
            def _():
                start = pl.multiple_of(b * LANES, LANES)
                columns = pl.ds(start, LANES)
                bases = [base_ref[b, k * 8 : k * 8 + 8, :] for k in range(row_groups)]

                def more(i, c):
                    moved_bases = [base + (i * TAPS).astype(jnp.float32) for base in bases]
                    rows_taken = tap_rows(moved_bases, 0, slab_ref[:, pl.ds(start, 2 * LANES)])
                    taken = (lambda i: rows_taken[i, :LANES]), (lambda i: rows_taken[i, LANES:])
                    for k in range(height // 16):
                        rows = slice(k * 16, k * 16 + 16)
                        mixed_ref[rows, columns] = mixed_ref[rows, columns] + render(
                            sample_ref[0, rows, columns],
                            sample_ref[1, rows, columns],
                            base_ref[b, rows, :] + (i * TAPS).astype(jnp.float32),
                            taken,
                            k,
                        )
                    return c

                lax.fori_loop(1, (widest + 1 + TAPS) // TAPS, more, 0)

            return carry

        lax.fori_loop(0, blocks, rest, 0)

    out_ref[...] = mixed_ref[...].astype(jnp.bfloat16)


def per_device(points, source, slab_first, slab_count):
    strips = lax.axis_size("ty")
    height, width = source.shape
    tile_len = points.shape[1]
    blocks = width // LANES
    in_chip = [(i, i ^ 1) for i in range(strips)]
    across = []
    for i in range(1, strips - 1, 2):
        across.extend([(i, i + 1), (i + 1, i)])
    vmem = pl.BlockSpec(memory_space=pltpu.VMEM)
    smem = pl.BlockSpec(memory_space=pltpu.SMEM)
    anywhere = pl.BlockSpec(memory_space=pl.ANY)
    params = pltpu.CompilerParams(vmem_limit_bytes=32 * 1024 * 1024)
    small = pltpu.CompilerParams(vmem_limit_bytes=4 * 1024 * 1024)
    mate_points = lax.ppermute(points, "ty", in_chip)
    packed_rows = width // tile_len * height + 16
    packed_shape = jax.ShapeDtypeStruct((packed_rows, tile_len), jnp.bfloat16)
    laid = pl.pallas_call(
        lay_source_kernel,
        out_shape=packed_shape,
        in_specs=[vmem],
        out_specs=vmem,
        compiler_params=small,
        cost_estimate=pl.CostEstimate(flops=0, bytes_accessed=4 * source.size, transcendentals=0),
    )(source)
    packed = pl.pallas_call(
        functools.partial(lay_points_kernel, height, width),
        out_shape=packed_shape,
        in_specs=[vmem, vmem, anywhere],
        out_specs=anywhere,
        input_output_aliases={2: 0},
        scratch_shapes=[pltpu.VMEM((16, tile_len), jnp.bfloat16), pltpu.SemaphoreType.DMA],
        compiler_params=small,
    )(points, mate_points, laid)
    arrived = lax.ppermute(packed, "ty", across)
    mate_source = lax.ppermute(source, "ty", in_chip)
    groups = width // GROUP_PX

    def moment_scratch(sets):
        length = sets * tile_len // groups
        return [
            pltpu.VMEM((groups, 2 * NF, length), jnp.bfloat16),
            pltpu.VMEM((groups, 2 * LANES, length), jnp.bfloat16),
        ]

    totals = pl.pallas_call(
        functools.partial(near_kernel, strips, height, width),
        out_shape=jax.ShapeDtypeStruct((groups, NF, LANES), jnp.float32),
        in_specs=[vmem, vmem],
        out_specs=vmem,
        scratch_shapes=moment_scratch(2),
        compiler_params=params,
        cost_estimate=pl.CostEstimate(flops=4 * NF * LANES * 2 * tile_len * 4, bytes_accessed=10**6, transcendentals=2 * tile_len * NV),
    )(points, mate_points)
    arrived, totals = lax.optimization_barrier((arrived, totals))
    far = lax.ppermute(arrived[packed_rows - 16 : packed_rows - 8], "ty", in_chip)
    return pl.pallas_call(
        functools.partial(main_kernel, strips),
        out_shape=(
            jax.ShapeDtypeStruct((height, width), jnp.bfloat16),
            jax.ShapeDtypeStruct((6, VR, width // SP), jnp.float32),
        ),
        in_specs=[smem, smem] + [vmem] * 5,
        out_specs=(vmem, vmem),
        scratch_shapes=moment_scratch(3)
        + [
            pltpu.VMEM((LANES, width + LANES), jnp.bfloat16),
            pltpu.VMEM((2, height, width), jnp.float32),
            pltpu.VMEM((blocks, height, LANES), jnp.float32),
            pltpu.VMEM((blocks, 8, LANES), jnp.float32),
            pltpu.VMEM((blocks, TAPS * height, 2 * LANES), jnp.bfloat16),
            pltpu.VMEM((height, width), jnp.float32),
            pltpu.SMEM((blocks,), jnp.int32),
        ],
        compiler_params=params,
    )(slab_first, slab_count, totals, source, mate_source, arrived, far)


def solution(mesh):
    return jax.shard_map(
        per_device,
        mesh=mesh,
        in_specs=(
            P(None, ("sec", "ty")),
            P(("sec", "ty"), None),
            P(("sec", "ty")),
            P(("sec", "ty")),
        ),
        out_specs=(P(("sec", "ty"), None), P(None, ("sec", "ty"), None)),
        check_vma=False,
    )
```

profile of v0, /device:TPU:7, one launch (start us, length us, event | category | flops | bytes accessed | tf_op | source)
XLA Modules:
  0.0 17.8 jit_solution(8227462239699498931)
XLA Ops:
  0.6 0.7 %collective-permute-start = (f32[4,1024]{1,0:T(4,128)}, f32[4,1024]{1,0:T(4,128)S(1)}, u32[]{:S(2)}, u32[]{:S(2)}) collective-permute-start(f32[4,1024]{1,0:T(4,128)} %own_ref.3), channel_id=1, source_target_pairs={{0,1},{1,0},{2,3},{3,2},{4,5},{5,4},{6,7},{7,6},{8,9},{9,8},{10,11... | collective-permute-start | bytes 49160 | tf_op jit(solution)/shard_map/ppermute | solution.py:432
  1.4 0.0 copy-start
  1.4 0.9 %copy-done = bf16[32,2048]{1,0:T(8,128)(2,1)S(1)} copy-done((bf16[32,2048]{1,0:T(8,128)(2,1)S(1)}, bf16[32,2048]{1,0:T(8,128)(2,1)}, u32[]{:S(2)}) %copy-start) | copy-done | bytes 131096
  2.3 0.0 copy-start.2
  2.3 0.0 copy-start.1
  2.3 0.1 collective-permute-done.mate_ref
  2.4 0.6 %copy-done.2 = f32[4,1024]{1,0:T(4,128)S(1)} copy-done((f32[4,1024]{1,0:T(4,128)S(1)}, f32[4,1024]{1,0:T(4,128)}, u32[]{:S(2)}) %copy-start.2) | copy-done | bytes 16408
  3.0 0.1 shard_map.60
  3.1 3.1 %collective-permute-start.1 = (bf16[80,1024]{1,0:T(8,128)(2,1)S(1)}, bf16[80,1024]{1,0:T(8,128)(2,1)S(1)}, u32[]{:S(2)}, u32[]{:S(2)}) collective-permute-start(bf16[80,1024]{1,0:T(8,128)(2,1)S(1)} %shard_map.60), channel_id=1, source_target_pairs={{1,2},{2,1},{3,4},{4,3},{5,6},{6,5},{7,8},{8,7},{9,10},{10,9},{11,... | collective-permute-start | bytes 491528 | tf_op jit(solution)/shard_map/ppermute | solution.py:452
  6.2 0.0 copy-done.1
  6.2 0.1 collective-permute-start.2
  6.3 0.8 %shard_map.61.totals_ref = f32[4,96,128]{2,1,0:T(8,128)S(1)} custom-call(f32[4,1024]{1,0:T(4,128)S(1)} %copy-done.2, f32[4,1024]{1,0:T(4,128)S(1)} %collective-permute-done.mate_ref), custom_call_target="tpu_custom_call" | custom-call | flops 402653184 | bytes 1000000 | tf_op jit(solution)/shard_map/pallas_call | solution.py:463
  7.1 3.6 %collective-permute-done.1.packed_ref = bf16[80,1024]{1,0:T(8,128)(2,1)S(1)} collective-permute-done((bf16[80,1024]{1,0:T(8,128)(2,1)S(1)}, bf16[80,1024]{1,0:T(8,128)(2,1)S(1)}, u32[]{:S(2)}, u32[]{:S(2)}) %collective-permute-start.1) | collective-permute-done | bytes 163872 | tf_op jit(solution)/shard_map/ppermute | solution.py:452
  10.7 0.8 %collective-permute-start.3 = (bf16[8,1024]{1,0:T(8,128)(2,1)S(1)}, bf16[8,1024]{1,0:T(8,128)(2,1)S(1)}, u32[]{:S(2)}, u32[]{:S(2)}) collective-permute-start(bf16[8,1024]{1,0:T(8,128)(2,1)S(1)} %slice.3), channel_id=1, source_target_pairs={{0,1},{1,0},{2,3},{3,2},{4,5},{5,4},{6,7},{7,6},{8,9},{9,8},{10,11... | collective-permute-start | bytes 49160 | tf_op jit(solution)/shard_map/ppermute | solution.py:473
  12.8 0.0 collective-permute-done.2.mate_source_ref
  12.8 0.0 collective-permute-done.3.far_ref
  12.8 4.9 %shard_map.62 = (bf16[32,2048]{1,0:T(8,128)(2,1)}, f32[6,4,256]{2,1,0:T(4,128)}) custom-call(s32[1]{0:T(128)S(6)} %copy.8.first_ref, s32[1]{0:T(128)S(6)} %copy.9.count_ref, f32[4,96,128]{2,1,0:T(8,128)S(1)} %shard_map.61.totals_ref, bf16[32,2048]{1,0:T(8,128)(2,1)S(1)} %copy-done.1, bf16[32,2048]{1,0:T(8,128)(2,1)S(1)} %collective-permute-done.2.mate_source_ref, ...), custom_call_target="tpu_custom_call" | custom-call | tf_op jit(solution)/shard_map/pallas_call | solution.py:474
  (2 shorter events, 0.0 us)
Async XLA Ops:
  0.6 1.8 %collective-permute-start = (f32[4,1024]{1,0:T(4,128)}, f32[4,1024]{1,0:T(4,128)S(1)}, u32[]{:S(2)}, u32[]{:S(2)}) collective-permute-start(f32[4,1024]{1,0:T(4,128)} %own_ref.3), channel_id=1, source_target_pairs={{0,1},{1,0},{2,3},{3,2},{4,5},{5,4},{6,7},{7,6},{8,9},{9,8},{10,11... | collective-permute-start | bytes 49160 | tf_op jit(solution)/shard_map/ppermute | solution.py:432
  1.4 0.9 %copy-start = (bf16[32,2048]{1,0:T(8,128)(2,1)S(1)}, bf16[32,2048]{1,0:T(8,128)(2,1)}, u32[]{:S(2)}) copy-start(bf16[32,2048]{1,0:T(8,128)(2,1)} %source_ref.3) | copy-start | bytes 393220
  2.3 0.7 %copy-start.2 = (f32[4,1024]{1,0:T(4,128)S(1)}, f32[4,1024]{1,0:T(4,128)}, u32[]{:S(2)}) copy-start(f32[4,1024]{1,0:T(4,128)} %own_ref.3) | copy-start | bytes 49156
  2.3 3.9 %copy-start.1 = (bf16[32,2048]{1,0:T(8,128)(2,1)S(1)}, bf16[32,2048]{1,0:T(8,128)(2,1)}, u32[]{:S(2)}) copy-start(bf16[32,2048]{1,0:T(8,128)(2,1)} %source_ref.3) | copy-start | bytes 393220
  3.1 7.6 %collective-permute-start.1 = (bf16[80,1024]{1,0:T(8,128)(2,1)S(1)}, bf16[80,1024]{1,0:T(8,128)(2,1)S(1)}, u32[]{:S(2)}, u32[]{:S(2)}) collective-permute-start(bf16[80,1024]{1,0:T(8,128)(2,1)S(1)} %shard_map.60), channel_id=1, source_target_pairs={{1,2},{2,1},{3,4},{4,3},{5,6},{6,5},{7,8},{8,7},{9,10},{10,9},{11,... | collective-permute-start | bytes 491528 | tf_op jit(solution)/shard_map/ppermute | solution.py:452
  6.2 6.6 %collective-permute-start.2 = (bf16[32,2048]{1,0:T(8,128)(2,1)S(1)}, bf16[32,2048]{1,0:T(8,128)(2,1)S(1)}, u32[]{:S(2)}, u32[]{:S(2)}) collective-permute-start(bf16[32,2048]{1,0:T(8,128)(2,1)S(1)} %copy-done.1), channel_id=1, source_target_pairs={{0,1},{1,0},{2,3},{3,2},{4,5},{5,4},{6,7},{7,6},{8,9},{9,8},{10,11... | collective-permute-start | bytes 393224 | tf_op jit(solution)/shard_map/ppermute | solution.py:453
  10.7 2.1 %collective-permute-start.3 = (bf16[8,1024]{1,0:T(8,128)(2,1)S(1)}, bf16[8,1024]{1,0:T(8,128)(2,1)S(1)}, u32[]{:S(2)}, u32[]{:S(2)}) collective-permute-start(bf16[8,1024]{1,0:T(8,128)(2,1)S(1)} %slice.3), channel_id=1, source_target_pairs={{0,1},{1,0},{2,3},{3,2},{4,5},{5,4},{6,7},{7,6},{8,9},{9,8},{10,11... | collective-permute-start | bytes 49160 | tf_op jit(solution)/shard_map/ppermute | solution.py:473
where the time goes:
time: 18 us; the launch traced here: 17.8 us
  Pallas kernels  5.86 us (33%)
  starting transfers between devices  4.65 us (26%)
  waiting for transfers between devices  3.76 us (21%)
  between operations  2 us (11%)
  local copies, waits for them, and re-layouts  1.49 us (8%)
    pallas_call x1, Pallas kernels, per_device(): pl.pallas_call(functools.partial(main_kernel, strips), out_shape=(jax.Sha...  4.92 us
    ppermute x1, waiting for transfers between devices, per_device(): arrived = lax.ppermute(packed, 'ty', across)  3.63 us
    ppermute x1, starting transfers between devices, per_device(): arrived = lax.ppermute(packed, 'ty', across)  3.08 us
    unnamed x6, local copies, waits for them, and re-layouts  1.48 us
    pallas_call x1, Pallas kernels, per_device(): pl.pallas_call(functools.partial(near_kernel, strips, height, width), out...  0.83 us
    ppermute x1, starting transfers between devices, per_device(): far = lax.ppermute(arrived[packed_rows - 16:packed_rows - 8], 'ty', in_chip)  0.77 us
    ppermute x1, starting transfers between devices, per_device(): mate_points = lax.ppermute(points, 'ty', in_chip)  0.74 us
  transfers between devices with their start and end apart: 4, of which 2 were waited for; matrix products, arithmetic and copies ran while one was open for 0% of the time, Pallas kernels for 5%

commit v1 on v0

--- a/solution.py
+++ b/solution.py
@@ -55,19 +55,22 @@
     return high, value - high
 
 
-def lay_source_kernel(source_ref, packed_ref):
+def shifts_of(local):
+    return jnp.concatenate([local[0:2], local[2:4] - local[0:2]], axis=0)
+
+
+def lay_own_kernel(local_ref, source_ref, packed_ref, rows_ref):
     height, width = source_ref.shape
     half = packed_ref.shape[1]
     for part in range(width // half):
         packed_ref[part * height : (part + 1) * height, :] = source_ref[:, part * half : (part + 1) * half]
-
-
-def lay_points_kernel(height, width, own_ref, mate_ref, laid_ref, packed_ref, rows_ref, sem):
+    rows_ref[...] = jnp.concatenate(split_pair(shifts_of(local_ref[...])), axis=0)
+
+
+def lay_mate_kernel(height, width, own_rows_ref, mate_ref, laid_ref, packed_ref, rows_ref, sem):
     tile = lax.axis_index("ty")
-    rows = []
-    for ref, owner in ((own_ref, tile), (mate_ref, tile + 1 - 2 * (tile % 2))):
-        rows.extend(split_pair(local_points(ref[...], owner, width // CELL, height)))
-    rows_ref[...] = jnp.concatenate(rows, axis=0).astype(jnp.bfloat16)
+    mate = split_pair(local_points(mate_ref[...], tile + 1 - 2 * (tile % 2), width // CELL, height))
+    rows_ref[...] = jnp.concatenate([own_rows_ref[...], *mate], axis=0).astype(jnp.bfloat16)
     base = packed_ref.shape[0] - 16
     copy = pltpu.make_async_copy(rows_ref, packed_ref.at[base : base + 16, :], sem)
     copy.start()
@@ -83,10 +86,23 @@
     ext_tile = tile + jnp.where(ext_row == 0, -1, jnp.where(ext_row == VR + 1, 1, 0))
     scale = float(np.sqrt(EXP2_SCALE))
     lane_px = (lax.broadcasted_iota(jnp.int32, (1, LANES), 1) // PC * CELL).astype(jnp.float32) - GROUP_PX / 2.0
-    vertex_ids = lax.broadcasted_iota(jnp.int32, (NV, LANES), 0)
-    point_block = lax.broadcasted_iota(jnp.int32, (NV, LANES), 1) // (LANES // CELL * PC)
-    band = (jnp.abs(vertex_ids // (LANES // SP) - 1 - point_block) <= 1).astype(jnp.float32)
-    vertex_scaled = (fiota((NV, 1), 0) * SP + (SP / 2.0 - LANES - GROUP_PX / 2.0)) * (scale / height)
+    per_block = LANES // SP
+    block_lanes = LANES // CELL * PC
+    reach = 3 * per_block
+    lane_ids = lax.broadcasted_iota(jnp.int32, (1, LANES), 1)
+    block_px = (lane_ids % block_lanes // PC * CELL).astype(jnp.float32) + (LANES - SP / 2.0)
+    vertex_px = fiota((reach, 1), 0) * SP
+    lane_block = (lax.broadcasted_iota(jnp.int32, (per_block, LANES), 1) // block_lanes).astype(jnp.int16)
+    in_block = [lane_block == j for j in range(LANES // block_lanes)]
+    nothing = jnp.zeros((per_block, LANES), jnp.bfloat16)
+
+    def spread_out(near, i):
+        result = nothing
+        for m in range(3):
+            if 0 <= i - m < len(in_block):
+                result = jnp.where(in_block[i - m], near[m * per_block : (m + 1) * per_block], result)
+        return result
+
     zero_rows = jnp.zeros((LANES - NV, weight_ref.shape[2]), jnp.bfloat16)
 
     totals = []
@@ -111,11 +127,12 @@
                     high, low = split_pair(jnp.concatenate(rows[f : f + 2], axis=0))
                     feat_ref[g, f * ER : (f + 2) * ER, chunk] = high.astype(jnp.bfloat16)
                     feat_ref[g, NF + f * ER : NF + (f + 2) * ER, chunk] = low.astype(jnp.bfloat16)
-                gap_x = px * scale - vertex_scaled
-                wx = jnp.exp2(-(gap_x * gap_x)) * band
-                high, low = split_pair(wx)
-                weight_ref[g, 0:NV, chunk] = high.astype(jnp.bfloat16)
-                weight_ref[g, LANES : LANES + NV, chunk] = low.astype(jnp.bfloat16)
+                gap_x = (pts[0:1, lanes] + block_px - vertex_px) * (scale / height)
+                high, low = split_pair(jnp.exp2(-(gap_x * gap_x)))
+                for row, near in ((0, high.astype(jnp.bfloat16)), (LANES, low.astype(jnp.bfloat16))):
+                    for i in range(NV // per_block):
+                        start = row + i * per_block
+                        weight_ref[g, start : start + per_block, chunk] = spread_out(near, i)
         both = lax.dot_general(
             feat_ref[g], weight_ref[g], (((1,), (1,)), ((), ())), preferred_element_type=jnp.float32
         )
@@ -129,7 +146,7 @@
     mate = tile + 1 - 2 * (tile % 2)
     cell_cols = width // CELL
     sets = (
-        (local_points(own_ref[...], tile, cell_cols, height), tile),
+        (shifts_of(own_ref[...]), tile),
         (local_points(mate_ref[...], mate, cell_cols, height), mate),
     )
     for g, value in enumerate(group_totals(sets, tile, strips, height, width, feat_ref, weight_ref)):
@@ -289,14 +306,12 @@
     def clipped_floor(sample_y):
         return jnp.clip(jnp.floor(sample_y), -2.0, last_row)
 
-    def one_hot(base, k, offset):
-        return jnp.where(lane_full - base == float(offset), 1.0, 0.0)
-
-    def tap_rows(bases, offset, slab):
-        picks = [
-            jnp.concatenate([one_hot(bases[k], k, offset + j) for k in range(len(bases))], axis=0).astype(jnp.bfloat16)
-            for j in range(TAPS)
-        ]
+    lanes_16 = fiota((16, LANES), 1)
+
+    def tap_rows(bases, slab):
+        away = [(lanes_16 - base).astype(jnp.int32).astype(jnp.int16) for base in bases]
+        one, none = jnp.ones((16, LANES), jnp.bfloat16), jnp.zeros((16, LANES), jnp.bfloat16)
+        picks = [jnp.where(gap == j, one, none) for j in range(TAPS) for gap in away]
         return jnp.dot(jnp.concatenate(picks, axis=0), slab, preferred_element_type=jnp.float32).astype(jnp.bfloat16)
 
     def render(sample_x, sample_y, base, taken, k):
@@ -365,8 +380,8 @@
 
     for b in range(blocks):
         columns = slice(b * LANES, (b + 1) * LANES)
-        bases = [base_ref[b, k * 8 : k * 8 + 8, :] for k in range(row_groups)]
-        taken_ref[b] = tap_rows(bases, 0, slab_ref[:, b * LANES : (b + 2) * LANES])
+        bases = [base_ref[b, k * 16 : k * 16 + 16, :] for k in range(height // 16)]
+        taken_ref[b] = tap_rows(bases, slab_ref[:, b * LANES : (b + 2) * LANES])
 
     for b in range(blocks):
         columns = slice(b * LANES, (b + 1) * LANES)
@@ -389,11 +404,11 @@
             def _():
                 start = pl.multiple_of(b * LANES, LANES)
                 columns = pl.ds(start, LANES)
-                bases = [base_ref[b, k * 8 : k * 8 + 8, :] for k in range(row_groups)]
+                bases = [base_ref[b, k * 16 : k * 16 + 16, :] for k in range(height // 16)]
 
                 def more(i, c):
                     moved_bases = [base + (i * TAPS).astype(jnp.float32) for base in bases]
-                    rows_taken = tap_rows(moved_bases, 0, slab_ref[:, pl.ds(start, 2 * LANES)])
+                    rows_taken = tap_rows(moved_bases, slab_ref[:, pl.ds(start, 2 * LANES)])
                     taken = (lambda i: rows_taken[i, :LANES]), (lambda i: rows_taken[i, LANES:])
                     for k in range(height // 16):
                         rows = slice(k * 16, k * 16 + 16)
@@ -432,23 +447,30 @@
     mate_points = lax.ppermute(points, "ty", in_chip)
     packed_rows = width // tile_len * height + 16
     packed_shape = jax.ShapeDtypeStruct((packed_rows, tile_len), jnp.bfloat16)
-    laid = pl.pallas_call(
-        lay_source_kernel,
-        out_shape=packed_shape,
-        in_specs=[vmem],
-        out_specs=vmem,
+    tile = lax.axis_index("ty")
+    cell = lax.broadcasted_iota(jnp.int32, points.shape, 1) // PC
+    cell_cols = width // CELL
+    origin_x = cell % cell_cols * CELL
+    origin_y = tile * height + cell // cell_cols * CELL
+    is_x = lax.broadcasted_iota(jnp.int32, points.shape, 0) % 2 == 0
+    local = points - jnp.where(is_x, origin_x, origin_y).astype(jnp.float32)
+    laid, own_rows = pl.pallas_call(
+        lay_own_kernel,
+        out_shape=(packed_shape, jax.ShapeDtypeStruct((8, tile_len), jnp.float32)),
+        in_specs=[vmem, vmem],
+        out_specs=(vmem, vmem),
         compiler_params=small,
         cost_estimate=pl.CostEstimate(flops=0, bytes_accessed=4 * source.size, transcendentals=0),
-    )(source)
+    )(local, source)
     packed = pl.pallas_call(
-        functools.partial(lay_points_kernel, height, width),
+        functools.partial(lay_mate_kernel, height, width),
         out_shape=packed_shape,
         in_specs=[vmem, vmem, anywhere],
         out_specs=anywhere,
         input_output_aliases={2: 0},
         scratch_shapes=[pltpu.VMEM((16, tile_len), jnp.bfloat16), pltpu.SemaphoreType.DMA],
         compiler_params=small,
-    )(points, mate_points, laid)
+    )(own_rows, mate_points, laid)
     arrived = lax.ppermute(packed, "ty", across)
     mate_source = lax.ppermute(source, "ty", in_chip)
     groups = width // GROUP_PX
@@ -468,7 +490,7 @@
         scratch_shapes=moment_scratch(2),
         compiler_params=params,
         cost_estimate=pl.CostEstimate(flops=4 * NF * LANES * 2 * tile_len * 4, bytes_accessed=10**6, transcendentals=2 * tile_len * NV),
-    )(points, mate_points)
+    )(local, mate_points)
     arrived, totals = lax.optimization_barrier((arrived, totals))
     far = lax.ppermute(arrived[packed_rows - 16 : packed_rows - 8], "ty", in_chip)
     return pl.pallas_call(

time: 18 us -> 17.9 us (level)
  starting transfers between devices: 4.65 us -> 5.82 us
  waiting for transfers between devices: 3.76 us -> 3.16 us
  local copies, waits for them, and re-layouts: 1.49 us -> 0.91 us
  Pallas kernels: 5.86 us -> 5.62 us
    ppermute x1, starting transfers between devices: 3.08 us -> 3.66 us  [per_device(): arrived = lax.ppermute(packed, 'ty', across)]
    ppermute x1, starting transfers between devices: 0.77 us -> 1.35 us  [per_device(): far = lax.ppermute(arrived[packed_rows - 16:packed_rows - 8], 'ty', in_chip)]
    unnamed x6, local copies, waits for them, and re-layouts: 1.48 us -> 0.91 us
    ppermute x1, waiting for transfers between devices: 3.63 us -> 3.15 us  [per_device(): arrived = lax.ppermute(packed, 'ty', across)]
  transfers between devices with their start and end apart: 4 -> 4, of which waited for: 2 -> 1; matrix products, arithmetic and copies ran while one was open for 0% -> 1% of each run, Pallas kernels for 5% -> 4%
where the time goes in v1:
time: 17.9 us; the launch traced here: 17.6 us
  starting transfers between devices  5.82 us (33%)
  Pallas kernels  5.62 us (31%)
  waiting for transfers between devices  3.16 us (18%)
  between operations  2.04 us (11%)
  local copies, waits for them, and re-layouts  0.91 us (5%)
    pallas_call x1, Pallas kernels, per_device(): pl.pallas_call(functools.partial(main_kernel, strips), out_shape=(jax.Sha...  4.77 us
    ppermute x1, starting transfers between devices, per_device(): arrived = lax.ppermute(packed, 'ty', across)  3.66 us
    ppermute x1, waiting for transfers between devices, per_device(): arrived = lax.ppermute(packed, 'ty', across)  3.15 us
    ppermute x1, starting transfers between devices, per_device(): far = lax.ppermute(arrived[packed_rows - 16:packed_rows - 8], 'ty', in_chip)  1.35 us
    unnamed x6, local copies, waits for them, and re-layouts  0.91 us
    ppermute x1, starting transfers between devices, per_device(): mate_points = lax.ppermute(points, 'ty', in_chip)  0.74 us
    pallas_call x1, Pallas kernels, per_device(): pl.pallas_call(functools.partial(near_kernel, strips, height, width), out...  0.73 us
  transfers between devices with their start and end apart: 4, of which 1 were waited for; matrix products, arithmetic and copies ran while one was open for 1% of the time, Pallas kernels for 4%

profile of v1, /device:TPU:7, one launch (start us, length us, event | category | flops | bytes accessed | tf_op | source)
XLA Modules:
  0.0 17.6 jit_solution(17988596950214122895)
XLA Ops:
  0.6 0.0 copy-start.2
  0.6 0.7 %collective-permute-start = (f32[4,1024]{1,0:T(4,128)}, f32[4,1024]{1,0:T(4,128)S(1)}, u32[]{:S(2)}, u32[]{:S(2)}) collective-permute-start(f32[4,1024]{1,0:T(4,128)} %param.4), channel_id=1, source_target_pairs={{0,1},{1,0},{2,3},{3,2},{4,5},{5,4},{6,7},{7,6},{8,9},{9,8},{10,11... | collective-permute-start | bytes 49160 | tf_op jit(solution)/shard_map/ppermute | solution.py:447
  1.4 0.0 copy-done.2
  1.4 0.1 fusion.3.local_ref.own_ref
  1.5 0.0 copy-start
  1.5 0.9 %copy-done = bf16[32,2048]{1,0:T(8,128)(2,1)S(1)} copy-done((bf16[32,2048]{1,0:T(8,128)(2,1)S(1)}, bf16[32,2048]{1,0:T(8,128)(2,1)}, u32[]{:S(2)}) %copy-start) | copy-done | bytes 131096
  2.4 0.0 collective-permute-done.mate_ref
  2.4 0.0 copy-start.1
  2.5 0.1 shard_map.60
  2.6 3.7 %collective-permute-start.1 = (bf16[80,1024]{1,0:T(8,128)(2,1)S(1)}, bf16[80,1024]{1,0:T(8,128)(2,1)S(1)}, u32[]{:S(2)}, u32[]{:S(2)}) collective-permute-start(bf16[80,1024]{1,0:T(8,128)(2,1)S(1)} %shard_map.60), channel_id=1, source_target_pairs={{1,2},{2,1},{3,4},{4,3},{5,6},{6,5},{7,8},{8,7},{9,10},{10,9},{11,... | collective-permute-start | bytes 491528 | tf_op jit(solution)/shard_map/ppermute | solution.py:474
  6.2 0.0 copy-done.1
  6.2 0.1 collective-permute-start.2
  6.3 0.7 %shard_map.61.totals_ref = f32[4,96,128]{2,1,0:T(8,128)S(1)} custom-call(f32[4,1024]{1,0:T(4,128)S(1)} %fusion.3.local_ref.own_ref, f32[4,1024]{1,0:T(4,128)S(1)} %collective-permute-done.mate_ref), custom_call_target="tpu_custom_call" | custom-call | flops 402653184 | bytes 1000000 | tf_op jit(solution)/shard_map/pallas_call | solution.py:485
  7.1 3.1 %collective-permute-done.1.packed_ref = bf16[80,1024]{1,0:T(8,128)(2,1)S(1)} collective-permute-done((bf16[80,1024]{1,0:T(8,128)(2,1)S(1)}, bf16[80,1024]{1,0:T(8,128)(2,1)S(1)}, u32[]{:S(2)}, u32[]{:S(2)}) %collective-permute-start.1) | collective-permute-done | bytes 163872 | tf_op jit(solution)/shard_map/ppermute | solution.py:474
  10.2 1.3 %collective-permute-start.3 = (bf16[8,1024]{1,0:T(8,128)(2,1)S(1)}, bf16[8,1024]{1,0:T(8,128)(2,1)S(1)}, u32[]{:S(2)}, u32[]{:S(2)}) collective-permute-start(bf16[8,1024]{1,0:T(8,128)(2,1)S(1)} %slice.3), channel_id=1, source_target_pairs={{0,1},{1,0},{2,3},{3,2},{4,5},{5,4},{6,7},{7,6},{8,9},{9,8},{10,11... | collective-permute-start | bytes 49160 | tf_op jit(solution)/shard_map/ppermute | solution.py:495
  12.8 0.0 collective-permute-done.2.mate_source_ref
  12.9 0.0 collective-permute-done.3.far_ref
  12.9 4.8 %shard_map.62 = (bf16[32,2048]{1,0:T(8,128)(2,1)}, f32[6,4,256]{2,1,0:T(4,128)}) custom-call(s32[1]{0:T(128)S(6)} %copy.8.first_ref, s32[1]{0:T(128)S(6)} %copy.9.count_ref, f32[4,96,128]{2,1,0:T(8,128)S(1)} %shard_map.61.totals_ref, bf16[32,2048]{1,0:T(8,128)(2,1)S(1)} %copy-done.1, bf16[32,2048]{1,0:T(8,128)(2,1)S(1)} %collective-permute-done.2.mate_source_ref, ...), custom_call_target="tpu_custom_call" | custom-call | tf_op jit(solution)/shard_map/pallas_call | solution.py:496
  (6 shorter events, 0.0 us)
Async XLA Ops:
  0.6 0.8 %copy-start.2 = (f32[4,1024]{1,0:T(4,128)S(1)}, f32[4,1024]{1,0:T(4,128)}, u32[]{:S(2)}) copy-start(f32[4,1024]{1,0:T(4,128)} %param.4) | copy-start | bytes 49156
  0.6 1.8 %collective-permute-start = (f32[4,1024]{1,0:T(4,128)}, f32[4,1024]{1,0:T(4,128)S(1)}, u32[]{:S(2)}, u32[]{:S(2)}) collective-permute-start(f32[4,1024]{1,0:T(4,128)} %param.4), channel_id=1, source_target_pairs={{0,1},{1,0},{2,3},{3,2},{4,5},{5,4},{6,7},{7,6},{8,9},{9,8},{10,11... | collective-permute-start | bytes 49160 | tf_op jit(solution)/shard_map/ppermute | solution.py:447
  1.5 0.9 %copy-start = (bf16[32,2048]{1,0:T(8,128)(2,1)S(1)}, bf16[32,2048]{1,0:T(8,128)(2,1)}, u32[]{:S(2)}) copy-start(bf16[32,2048]{1,0:T(8,128)(2,1)} %source_ref.3) | copy-start | bytes 393220
  2.4 3.8 %copy-start.1 = (bf16[32,2048]{1,0:T(8,128)(2,1)S(1)}, bf16[32,2048]{1,0:T(8,128)(2,1)}, u32[]{:S(2)}) copy-start(bf16[32,2048]{1,0:T(8,128)(2,1)} %source_ref.3) | copy-start | bytes 393220
  2.6 7.6 %collective-permute-start.1 = (bf16[80,1024]{1,0:T(8,128)(2,1)S(1)}, bf16[80,1024]{1,0:T(8,128)(2,1)S(1)}, u32[]{:S(2)}, u32[]{:S(2)}) collective-permute-start(bf16[80,1024]{1,0:T(8,128)(2,1)S(1)} %shard_map.60), channel_id=1, source_target_pairs={{1,2},{2,1},{3,4},{4,3},{5,6},{6,5},{7,8},{8,7},{9,10},{10,9},{11,... | collective-permute-start | bytes 491528 | tf_op jit(solution)/shard_map/ppermute | solution.py:474
  6.2 6.6 %collective-permute-start.2 = (bf16[32,2048]{1,0:T(8,128)(2,1)S(1)}, bf16[32,2048]{1,0:T(8,128)(2,1)S(1)}, u32[]{:S(2)}, u32[]{:S(2)}) collective-permute-start(bf16[32,2048]{1,0:T(8,128)(2,1)S(1)} %copy-done.1), channel_id=1, source_target_pairs={{0,1},{1,0},{2,3},{3,2},{4,5},{5,4},{6,7},{7,6},{8,9},{9,8},{10,11... | collective-permute-start | bytes 393224 | tf_op jit(solution)/shard_map/ppermute | solution.py:475
  10.2 2.7 %collective-permute-start.3 = (bf16[8,1024]{1,0:T(8,128)(2,1)S(1)}, bf16[8,1024]{1,0:T(8,128)(2,1)S(1)}, u32[]{:S(2)}, u32[]{:S(2)}) collective-permute-start(bf16[8,1024]{1,0:T(8,128)(2,1)S(1)} %slice.3), channel_id=1, source_target_pairs={{0,1},{1,0},{2,3},{3,2},{4,5},{5,4},{6,7},{7,6},{8,9},{9,8},{10,11... | collective-permute-start | bytes 49160 | tf_op jit(solution)/shard_map/ppermute | solution.py:495

commit v2 on v1

--- a/solution.py
+++ b/solution.py
@@ -21,7 +21,7 @@
 GROUP_PX = LANES // PC * CELL
 NV = GROUP_PX // SP + 2 * LANES // SP
 EXP2_SCALE = 2.0 * float(np.log2(np.e))
-TAPS = 12
+TAPS = 13
 
 
 def fiota(shape, dim):

time: 17.9 us -> 18.2 us (1.017)
  Pallas kernels: 5.62 us -> 5.88 us
    pallas_call x1, Pallas kernels: 4.77 us -> 5.03 us  [per_device(): pl.pallas_call(functools.partial(main_kernel, strips), out_shape=(jax.Sha...]
where the time goes in v2:
time: 18.2 us; the launch traced here: 17.9 us
  Pallas kernels  5.88 us (32%)
  starting transfers between devices  5.82 us (32%)
  waiting for transfers between devices  3.16 us (17%)
  between operations  2.04 us (11%)
  local copies, waits for them, and re-layouts  0.91 us (5%)
    pallas_call x1, Pallas kernels, per_device(): pl.pallas_call(functools.partial(main_kernel, strips), out_shape=(jax.Sha...  5.03 us
    ppermute x1, starting transfers between devices, per_device(): arrived = lax.ppermute(packed, 'ty', across)  3.66 us
    ppermute x1, waiting for transfers between devices, per_device(): arrived = lax.ppermute(packed, 'ty', across)  3.15 us
    ppermute x1, starting transfers between devices, per_device(): far = lax.ppermute(arrived[packed_rows - 16:packed_rows - 8], 'ty', in_chip)  1.35 us
    unnamed x6, local copies, waits for them, and re-layouts  0.91 us
    ppermute x1, starting transfers between devices, per_device(): mate_points = lax.ppermute(points, 'ty', in_chip)  0.74 us
    pallas_call x1, Pallas kernels, per_device(): pl.pallas_call(functools.partial(near_kernel, strips, height, width), out...  0.73 us
  transfers between devices with their start and end apart: 4, of which 1 were waited for; matrix products, arithmetic and copies ran while one was open for 1% of the time, Pallas kernels for 4%

profile of v2, /device:TPU:7, one launch (start us, length us, event | category | flops | bytes accessed | tf_op | source)
XLA Modules:
  0.0 17.9 jit_solution(11288554374557613607)
XLA Ops:
  0.6 0.0 copy-start.2
  0.6 0.7 %collective-permute-start = (f32[4,1024]{1,0:T(4,128)}, f32[4,1024]{1,0:T(4,128)S(1)}, u32[]{:S(2)}, u32[]{:S(2)}) collective-permute-start(f32[4,1024]{1,0:T(4,128)} %param.4), channel_id=1, source_target_pairs={{0,1},{1,0},{2,3},{3,2},{4,5},{5,4},{6,7},{7,6},{8,9},{9,8},{10,11... | collective-permute-start | bytes 49160 | tf_op jit(solution)/shard_map/ppermute | solution.py:447
  1.4 0.0 copy-done.2
  1.4 0.1 fusion.3.local_ref.own_ref
  1.5 0.0 copy-start
  1.5 0.9 %copy-done = bf16[32,2048]{1,0:T(8,128)(2,1)S(1)} copy-done((bf16[32,2048]{1,0:T(8,128)(2,1)S(1)}, bf16[32,2048]{1,0:T(8,128)(2,1)}, u32[]{:S(2)}) %copy-start) | copy-done | bytes 131096
  2.4 0.0 collective-permute-done.mate_ref
  2.4 0.0 copy-start.1
  2.5 0.1 shard_map.60
  2.6 3.7 %collective-permute-start.1 = (bf16[80,1024]{1,0:T(8,128)(2,1)S(1)}, bf16[80,1024]{1,0:T(8,128)(2,1)S(1)}, u32[]{:S(2)}, u32[]{:S(2)}) collective-permute-start(bf16[80,1024]{1,0:T(8,128)(2,1)S(1)} %shard_map.60), channel_id=1, source_target_pairs={{1,2},{2,1},{3,4},{4,3},{5,6},{6,5},{7,8},{8,7},{9,10},{10,9},{11,... | collective-permute-start | bytes 491528 | tf_op jit(solution)/shard_map/ppermute | solution.py:474
  6.2 0.0 copy-done.1
  6.2 0.1 collective-permute-start.2
  6.3 0.7 %shard_map.61.totals_ref = f32[4,96,128]{2,1,0:T(8,128)S(1)} custom-call(f32[4,1024]{1,0:T(4,128)S(1)} %fusion.3.local_ref.own_ref, f32[4,1024]{1,0:T(4,128)S(1)} %collective-permute-done.mate_ref), custom_call_target="tpu_custom_call" | custom-call | flops 402653184 | bytes 1000000 | tf_op jit(solution)/shard_map/pallas_call | solution.py:485
  7.1 3.1 %collective-permute-done.1.packed_ref = bf16[80,1024]{1,0:T(8,128)(2,1)S(1)} collective-permute-done((bf16[80,1024]{1,0:T(8,128)(2,1)S(1)}, bf16[80,1024]{1,0:T(8,128)(2,1)S(1)}, u32[]{:S(2)}, u32[]{:S(2)}) %collective-permute-start.1) | collective-permute-done | bytes 163872 | tf_op jit(solution)/shard_map/ppermute | solution.py:474
  10.2 1.3 %collective-permute-start.3 = (bf16[8,1024]{1,0:T(8,128)(2,1)S(1)}, bf16[8,1024]{1,0:T(8,128)(2,1)S(1)}, u32[]{:S(2)}, u32[]{:S(2)}) collective-permute-start(bf16[8,1024]{1,0:T(8,128)(2,1)S(1)} %slice.3), channel_id=1, source_target_pairs={{0,1},{1,0},{2,3},{3,2},{4,5},{5,4},{6,7},{7,6},{8,9},{9,8},{10,11... | collective-permute-start | bytes 49160 | tf_op jit(solution)/shard_map/ppermute | solution.py:495
  12.8 0.0 collective-permute-done.2.mate_source_ref
  12.9 0.0 collective-permute-done.3.far_ref
  12.9 5.0 %shard_map.62 = (bf16[32,2048]{1,0:T(8,128)(2,1)}, f32[6,4,256]{2,1,0:T(4,128)}) custom-call(s32[1]{0:T(128)S(6)} %copy.8.first_ref, s32[1]{0:T(128)S(6)} %copy.9.count_ref, f32[4,96,128]{2,1,0:T(8,128)S(1)} %shard_map.61.totals_ref, bf16[32,2048]{1,0:T(8,128)(2,1)S(1)} %copy-done.1, bf16[32,2048]{1,0:T(8,128)(2,1)S(1)} %collective-permute-done.2.mate_source_ref, ...), custom_call_target="tpu_custom_call" | custom-call | tf_op jit(solution)/shard_map/pallas_call | solution.py:496
  (6 shorter events, 0.0 us)
Async XLA Ops:
  0.6 0.8 %copy-start.2 = (f32[4,1024]{1,0:T(4,128)S(1)}, f32[4,1024]{1,0:T(4,128)}, u32[]{:S(2)}) copy-start(f32[4,1024]{1,0:T(4,128)} %param.4) | copy-start | bytes 49156
  0.6 1.8 %collective-permute-start = (f32[4,1024]{1,0:T(4,128)}, f32[4,1024]{1,0:T(4,128)S(1)}, u32[]{:S(2)}, u32[]{:S(2)}) collective-permute-start(f32[4,1024]{1,0:T(4,128)} %param.4), channel_id=1, source_target_pairs={{0,1},{1,0},{2,3},{3,2},{4,5},{5,4},{6,7},{7,6},{8,9},{9,8},{10,11... | collective-permute-start | bytes 49160 | tf_op jit(solution)/shard_map/ppermute | solution.py:447
  1.5 0.9 %copy-start = (bf16[32,2048]{1,0:T(8,128)(2,1)S(1)}, bf16[32,2048]{1,0:T(8,128)(2,1)}, u32[]{:S(2)}) copy-start(bf16[32,2048]{1,0:T(8,128)(2,1)} %source_ref.3) | copy-start | bytes 393220
  2.4 3.8 %copy-start.1 = (bf16[32,2048]{1,0:T(8,128)(2,1)S(1)}, bf16[32,2048]{1,0:T(8,128)(2,1)}, u32[]{:S(2)}) copy-start(bf16[32,2048]{1,0:T(8,128)(2,1)} %source_ref.3) | copy-start | bytes 393220
  2.6 7.6 %collective-permute-start.1 = (bf16[80,1024]{1,0:T(8,128)(2,1)S(1)}, bf16[80,1024]{1,0:T(8,128)(2,1)S(1)}, u32[]{:S(2)}, u32[]{:S(2)}) collective-permute-start(bf16[80,1024]{1,0:T(8,128)(2,1)S(1)} %shard_map.60), channel_id=1, source_target_pairs={{1,2},{2,1},{3,4},{4,3},{5,6},{6,5},{7,8},{8,7},{9,10},{10,9},{11,... | collective-permute-start | bytes 491528 | tf_op jit(solution)/shard_map/ppermute | solution.py:474
  6.2 6.6 %collective-permute-start.2 = (bf16[32,2048]{1,0:T(8,128)(2,1)S(1)}, bf16[32,2048]{1,0:T(8,128)(2,1)S(1)}, u32[]{:S(2)}, u32[]{:S(2)}) collective-permute-start(bf16[32,2048]{1,0:T(8,128)(2,1)S(1)} %copy-done.1), channel_id=1, source_target_pairs={{0,1},{1,0},{2,3},{3,2},{4,5},{5,4},{6,7},{7,6},{8,9},{9,8},{10,11... | collective-permute-start | bytes 393224 | tf_op jit(solution)/shard_map/ppermute | solution.py:475
  10.2 2.7 %collective-permute-start.3 = (bf16[8,1024]{1,0:T(8,128)(2,1)S(1)}, bf16[8,1024]{1,0:T(8,128)(2,1)S(1)}, u32[]{:S(2)}, u32[]{:S(2)}) collective-permute-start(bf16[8,1024]{1,0:T(8,128)(2,1)S(1)} %slice.3), channel_id=1, source_target_pairs={{0,1},{1,0},{2,3},{3,2},{4,5},{5,4},{6,7},{7,6},{8,9},{9,8},{10,11... | collective-permute-start | bytes 49160 | tf_op jit(solution)/shard_map/ppermute | solution.py:495
